TPU v7x, 512 devices: a whole 4x8x8 slice. The times are simulated.
512 devices in a mesh: dom: 128 (over y, z, core), src: 4 (over x).
Axes of the slice: x: 4, y: 8, z: 8, core: 2. Of those that a mesh axis runs over, the one named last changes fastest.
Arguments:
- adjoint_dofs: float32 [4, 9, 56, 16384], P('src', None, None, 'dom'), may hold values from -6 to 6
- forward_dofs: bfloat16 [4, 9, 56, 16384], P('src', None, None, 'dom'), may hold values from -6 to 6
- star_matrices: float32 [3, 9, 9, 16384], P(None, None, None, 'dom'), may hold values from -3 to 3
- flux_matrices: float32 [4, 2, 9, 9, 16384], P(None, None, None, None, 'dom'), may hold values from -1.5 to 1.5
- stiffness: float32 [3, 56, 56], replicated, may hold values from -0.75 to 0.75
- restriction: float32 [4, 56, 21], replicated, may hold values from -0.75 to 0.75
- rotation: float32 [3, 21, 21], replicated, may hold values from -1.25 to 1.25
- lifting: float32 [4, 21, 56], replicated, may hold values from -0.625 to 0.625
- kernel_weights: float32 [3, 9, 9], replicated, may hold values from -0.046875 to 0.046875
- neighbour: int32 [4, 16384], P(None, 'dom'), may hold values from -1 to 703
- send_face: int32 [6, 4096], P(None, 'dom'), may hold values from -1 to 511, as said below
- orientation: int32 [4, 16384], P(None, 'dom'), may hold values from 0 to 2
- cluster: int32 [16384], P('dom'), may hold values from 0 to 1
- model_cell: int32 [16384], P('dom'), may hold values from 0 to 16383, as said below
Outputs:
- adjoint_next: float32 [4, 9, 56, 16384], P('src', None, None, 'dom')
- model_gradient: float32 [3, 16384], P(None, 'dom')
Inputs may be any that keep to these rules, and one draw needn't show every extreme that they name: Faces are paired both ways, and every such slot is listed by the sending partition. `send_face`: row k < 3 of partition p lists in slot c the own face h * 128 + e that borders partition p + k + 1, row 3 + k those bordering p - k - 1; unused slots hold -1. Partition 0 fills all 32 slots of each of its upward rows, and partition 128 - 1 all of each of its downward rows. `model_cell`: the cell of an element of partition p is owned by partition cell // 128, which lies within p - 3 to p + 3; every partition holds elements whose cells are owned by each partition of that range that lies in the slab.
All inputs are finite; a program needn't handle non-finite values.
Results may differ from a plain program's by a relative error of at most 0.0003.
Values sent between devices are 32-bit elements; how exact they have to be, the bound alone decides.
A program may use at most 128 MiB of HBM per device.

v0:
```python
import functools

import jax
import jax.numpy as jnp
from jax import lax
from jax.experimental import pallas as pl
from jax.experimental.pallas import tpu as pltpu
from jax.sharding import PartitionSpec as P

MESH = pl.DeviceIdType.MESH
F32 = jnp.float32
BF16 = jnp.bfloat16

Q = 9
B = 56
BP = 64
F = 21
FP = 24
E = 128
NF = 4
FACES = NF * E
ROWS = 224
QP = Q * FP
PARAMS = 3


def halves(x):
    high = x.astype(BF16).astype(F32)
    return high, x - high


def nt_dot(a, b):
    return lax.dot_general(a, b, (((1,), (1,)), ((), ())), preferred_element_type=F32)


def nn_dot(a, b):
    return jnp.dot(a, b, preferred_element_type=F32)


def kernel(
    n_dom,
    n_src,
    reach,
    cap,
    adj_ref,
    fwd_ref,
    star_ref,
    flux_hbm,
    stiff_ref,
    restr_ref,
    rot_ref,
    lift_ref,
    kw_ref,
    nbr_ref,
    send_ref,
    orient_ref,
    clus_ref,
    cell_ref,
    out_ref,
    grad_ref,
    flux_ref,
    build,
    wk,
    wv,
    wt,
    rb,
    lw,
    v3,
    applied,
    integral,
    fwd32,
    pool,
    pcat,
    oh,
    ohs,
    gath,
    xg,
    turned,
    ft,
    ftb,
    base,
    sendbuf,
    recvbuf,
    sendwin,
    recvwin,
    sendsum,
    recvsum,
    flux_sem,
    send_sem,
    recv_sem,
    wsend_sem,
    wrecv_sem,
    ssend_sem,
    srecv_sem,
):
    dom = lax.axis_index("dom")
    src = lax.axis_index("src")
    slots = 2 * reach
    up = [lax.rem(dom + (k + 1), n_dom) for k in range(reach)]
    down = [lax.rem(dom + (n_dom - k - 1), n_dom) for k in range(reach)]
    partners = up + down
    others = [lax.rem(src + (s + 1), n_src) for s in range(n_src - 1)]

    flux_copy = pltpu.make_async_copy(flux_hbm, flux_ref, flux_sem)
    flux_copy.start()

    barrier = pltpu.get_barrier_semaphore()
    for partner in partners:
        pl.semaphore_signal(barrier, inc=1, device_id={"dom": partner}, device_id_type=MESH)
    for other in others:
        pl.semaphore_signal(barrier, inc=1, device_id={"src": other}, device_id_type=MESH)

    build[...] = jnp.zeros_like(build)
    for d in range(3):
        high, low = halves(stiff_ref[d])
        build[d * B : (d + 1) * B, 0:B] = high
        build[d * B : (d + 1) * B, BP : BP + B] = high
        build[d * B : (d + 1) * B, 2 * BP : 2 * BP + B] = low
    wk[...] = build[0 : 3 * B, 0 : 3 * BP].astype(BF16)

    zeros8 = jnp.zeros((BP - B, E), F32)

    def put_state(q, value):
        high, low = halves(jnp.concatenate([value, zeros8], axis=0))
        lanes = pl.ds(pl.multiple_of(q * E, E), E)
        v3[0:BP, lanes] = high.astype(BF16)
        v3[BP : 2 * BP, lanes] = low.astype(BF16)
        v3[2 * BP : 3 * BP, lanes] = high.astype(BF16)

    def start_state(q, carry):
        value = adj_ref[0, q]
        integral[q] = value
        put_state(q, value)
        return carry

    lax.fori_loop(0, Q, start_state, 0)

    def multiply(weights):
        for tile in range(5):
            lanes = slice(tile * 256, min(tile * 256 + 256, Q * E))
            applied[:, lanes] = nn_dot(weights[...], v3[:, lanes])

    def contract(block, finish):
        p0 = block * 3
        totals = [None] * 3
        for q in range(Q):
            for d in range(3):
                a = applied[d * B : (d + 1) * B, q * E : (q + 1) * E]
                for i in range(3):
                    term = star_ref[p0 + i, q, d : d + 1, :] * a
                    totals[i] = term if totals[i] is None else totals[i] + term
        for i in range(3):
            finish(p0 + i, totals[i])

    def degree_step(k, carry):
        multiply(wk)
        scale = jnp.float32(-1.0 / 6.0)
        for n in range(4):
            scale = jnp.where(k == n, jnp.float32(-1.0 / (n + 2)), scale)

        def finish(p, total):
            value = total * scale
            integral[p] = integral[p] + value
            put_state(p, value)

        def block_step(block, c):
            contract(block, finish)
            return c

        lax.fori_loop(0, 3, block_step, 0)
        return carry

    lax.fori_loop(0, 5, degree_step, 0)

    def take_integral(q, carry):
        put_state(q, integral[q])
        return carry

    lax.fori_loop(0, Q, take_integral, 0)

    build[...] = jnp.zeros_like(build)
    for j in range(NF):
        high, low = halves(restr_ref[:, j, :])
        build[j * FP : j * FP + F, 0:B] = high
        build[j * FP : j * FP + F, BP : BP + B] = high
        build[j * FP : j * FP + F, 2 * BP : 2 * BP + B] = low
    wt[...] = build[0 : NF * FP, 0 : 3 * BP].astype(BF16)
    pool[QP:ROWS, :] = jnp.zeros((ROWS - QP, FACES), F32)
    for tile in range(5):
        wide = min(2, Q - 2 * tile)
        result = nn_dot(wt[...], v3[:, tile * 256 : tile * 256 + wide * E])
        for i in range(wide):
            q = 2 * tile + i
            for j in range(NF):
                pool[q * FP : (q + 1) * FP, j * E : (j + 1) * E] = result[
                    j * FP : (j + 1) * FP, i * E : (i + 1) * E
                ]
    high, low = halves(pool[...])
    pcat[:, 0:FACES] = high.astype(BF16)
    pcat[:, FACES : 2 * FACES] = low.astype(BF16)

    listed = send_ref[...].astype(F32).T
    face_lane = lax.broadcasted_iota(jnp.int32, (cap, FACES), 1).astype(F32)
    for k in range(slots):
        hit = listed[:, k : k + 1] == face_lane
        ohs[k * cap : (k + 1) * cap, :] = jnp.where(hit, 1.0, 0.0).astype(BF16)
    sendbuf[...] = nt_dot(ohs[...], pcat[:, 0:FACES]) + nt_dot(ohs[...], pcat[:, FACES : 2 * FACES])

    pl.semaphore_wait(barrier, 2 * reach + n_src - 1)

    def trace_copy(k):
        part = pl.ds(k * cap, cap)
        return pltpu.make_async_remote_copy(
            src_ref=sendbuf.at[part],
            dst_ref=recvbuf.at[part],
            send_sem=send_sem.at[k],
            recv_sem=recv_sem.at[k],
            device_id={"dom": partners[k]},
            device_id_type=MESH,
        )

    for k in range(slots):
        trace_copy(k).start()

    fwd32[...] = fwd_ref[0].astype(F32)

    def pair_step(q, carry):
        own = integral[q]
        sums = list(carry)
        for r in range(Q):
            product = own * fwd32[r]
            pair = product[0:8]
            for c in range(1, 7):
                pair = pair + product[8 * c : 8 * c + 8]
            for n in range(PARAMS):
                sums[n] = sums[n] + kw_ref[q, n, r] * pair
        return tuple(sums)

    sums = lax.fori_loop(0, Q, pair_step, tuple(jnp.zeros((8, E), F32) for _ in range(PARAMS)))
    terms = jnp.concatenate(
        [jnp.sum(s, axis=0, keepdims=True) for s in sums] + [jnp.zeros((8 - PARAMS, E), F32)], axis=0
    )
    high, low = halves(terms)
    both = jnp.concatenate([high, low], axis=0).astype(BF16)
    place = cell_ref[...] - (dom - reach) * E
    for o in range(2 * reach + 1):
        row = lax.broadcasted_iota(jnp.int32, (E, E), 0) + o * E
        hit = jnp.where(row == place, 1.0, 0.0).astype(BF16)
        summed = nt_dot(both, hit)
        sendwin[o] = summed[0:8] + summed[8:16]

    def window_copy(k):
        o = reach + k + 1 if k < reach else 2 * reach - 1 - k
        return pltpu.make_async_remote_copy(
            src_ref=sendwin.at[o],
            dst_ref=recvwin.at[k],
            send_sem=wsend_sem.at[k],
            recv_sem=wrecv_sem.at[k],
            device_id={"dom": partners[k]},
            device_id_type=MESH,
        )

    for k in range(slots):
        window_copy(k).start()

    flux_copy.wait()

    def flux_side(j, side, values, finish):
        lanes = pl.ds(pl.multiple_of(j * E, E), E)
        x = [values[q * FP : (q + 1) * FP, lanes] for q in range(Q)]
        for p in range(Q):
            total = None
            for q in range(Q):
                term = flux_ref[j, p, q, side : side + 1, :] * x[q]
                total = term if total is None else total + term
            finish(j, p, total)

    def own_step(j, carry):
        def finish(j, p, total):
            ft[pl.ds(pl.multiple_of(j * FP, FP), FP), p * E : (p + 1) * E] = total

        flux_side(j, 0, pool, finish)
        return carry

    lax.fori_loop(0, NF, own_step, 0)

    build[...] = jnp.zeros_like(build)
    for d in range(3):
        high, low = halves(stiff_ref[d].T)
        build[d * B : (d + 1) * B, 0:B] = high
        build[d * B : (d + 1) * B, BP : BP + B] = high
        build[d * B : (d + 1) * B, 2 * BP : 2 * BP + B] = low
    wv[...] = build[0 : 3 * B, 0 : 3 * BP].astype(BF16)
    multiply(wv)

    def volume_step(block, carry):
        def finish(p, total):
            base[p] = adj_ref[0, p] + total

        contract(block, finish)
        return carry

    lax.fori_loop(0, 3, volume_step, 0)

    for j in range(NF):
        row = lax.broadcasted_iota(jnp.int32, (FACES + slots * cap, E), 0)
        hit = row == nbr_ref[j : j + 1, :]
        oh[:, j * E : (j + 1) * E] = jnp.where(hit, 1.0, 0.0).astype(BF16)
    gath[...] = nn_dot(pcat[:, 0:FACES], oh[0:FACES, :]) + nn_dot(pcat[:, FACES : 2 * FACES], oh[0:FACES, :])

    build[...] = jnp.zeros_like(build)
    for o in range(3):
        high, low = halves(rot_ref[o])
        for i in range(3):
            rows = slice(i * 72 + o * FP, i * 72 + o * FP + F)
            build[rows, i * 72 : i * 72 + F] = high
            build[rows, i * 72 + FP : i * 72 + FP + F] = high
            build[rows, i * 72 + 2 * FP : i * 72 + 2 * FP + F] = low
    rb[...] = build[0:QP, 0:ROWS].astype(BF16)
    build[...] = jnp.zeros_like(build)
    for j in range(NF):
        high, low = halves(lift_ref[:, j, :].T)
        build[0:B, j * FP : j * FP + F] = high
        build[0:B, NF * FP + j * FP : NF * FP + j * FP + F] = high
        build[B : 2 * B, j * FP : j * FP + F] = low
    lw[...] = build[0 : 2 * B, 0 : 2 * NF * FP].astype(BF16)

    for k in range(slots):
        window_copy(k).wait_recv()
    total = sendwin[reach]
    for k in range(slots):
        total = total + recvwin[k]
    sendsum[...] = total

    def sum_copy(s):
        return pltpu.make_async_remote_copy(
            src_ref=sendsum,
            dst_ref=recvsum.at[s],
            send_sem=ssend_sem.at[s],
            recv_sem=srecv_sem.at[s],
            device_id={"src": others[s]},
            device_id_type=MESH,
        )

    for s in range(n_src - 1):
        sum_copy(s).start()

    for k in range(slots):
        trace_copy(k).wait_recv()
    high, low = halves(recvbuf[...].T)
    far = oh[FACES : FACES + slots * cap, :]
    gath[...] = gath[...] + nn_dot(high.astype(BF16), far) + nn_dot(low.astype(BF16), far)

    xg[QP:ROWS, :] = jnp.zeros((ROWS - QP, FACES), F32)
    for t in range(3):
        for i in range(3):
            q = 3 * t + i
            high, low = halves(gath[q * FP : (q + 1) * FP, :])
            xg[i * 72 : i * 72 + FP, :] = high
            xg[i * 72 + FP : i * 72 + 2 * FP, :] = low
            xg[i * 72 + 2 * FP : i * 72 + 3 * FP, :] = high
        result = nn_dot(rb[...], xg[...].astype(BF16))
        for i in range(3):
            q = 3 * t + i
            for j in range(NF):
                o = orient_ref[j : j + 1, :]
                r = [
                    result[i * 72 + n * FP : i * 72 + (n + 1) * FP, j * E : (j + 1) * E] for n in range(3)
                ]
                turned[q * FP : (q + 1) * FP, j * E : (j + 1) * E] = jnp.where(
                    o == 0, r[0], jnp.where(o == 1, r[1], r[2])
                )

    def far_step(j, carry):
        def finish(j, p, total):
            rows = pl.ds(pl.multiple_of(j * FP, FP), FP)
            lanes = slice(p * E, (p + 1) * E)
            ft[rows, lanes] = ft[rows, lanes] + total

        flux_side(j, 1, turned, finish)
        return carry

    lax.fori_loop(0, NF, far_step, 0)

    high, low = halves(ft[...])
    ftb[0 : NF * FP, :] = high.astype(BF16)
    ftb[NF * FP : 2 * NF * FP, :] = low.astype(BF16)
    moves = clus_ref[...] == 0
    for tile in range(5):
        wide = min(2, Q - 2 * tile)
        result = nn_dot(lw[...], ftb[:, tile * 256 : tile * 256 + wide * E])
        surface = result[0:B] + result[B : 2 * B]
        for i in range(wide):
            p = 2 * tile + i
            out_ref[0, p] = jnp.where(moves, base[p] - surface[:, i * E : (i + 1) * E], adj_ref[0, p])

    for s in range(n_src - 1):
        sum_copy(s).wait_recv()
    total = sendsum[...]
    for s in range(n_src - 1):
        total = total + recvsum[s]
    grad_ref[...] = total[0:PARAMS]

    for k in range(slots):
        trace_copy(k).wait_send()
        window_copy(k).wait_send()
    for s in range(n_src - 1):
        sum_copy(s).wait_send()


def solution(mesh):
    n_dom, n_src = mesh.shape["dom"], mesh.shape["src"]

    def body(adj, fwd, star, flux, stiff, restr, rot, lift, kw, nbr, send, orient, clus, cell):
        reach, cap = send.shape[0] // 2, send.shape[1]
        star = star.transpose(1, 2, 0, 3)
        flux = flux.transpose(0, 2, 3, 1, 4)
        restr = restr.transpose(2, 0, 1)
        lift = lift.transpose(1, 0, 2)
        kw = kw.transpose(1, 0, 2)
        slots = 2 * reach
        vmem = pl.BlockSpec(memory_space=pltpu.VMEM)
        specs = [vmem] * 14
        specs[3] = pl.BlockSpec(memory_space=pl.ANY)
        specs[8] = pl.BlockSpec(memory_space=pltpu.SMEM)
        dma = pltpu.SemaphoreType.DMA
        return pl.pallas_call(
            functools.partial(kernel, n_dom, n_src, reach, cap),
            out_shape=(
                jax.ShapeDtypeStruct(adj.shape, F32),
                jax.ShapeDtypeStruct((PARAMS, E), F32),
            ),
            in_specs=specs,
            out_specs=(vmem, vmem),
            scratch_shapes=[
                pltpu.VMEM(flux.shape, F32),
                pltpu.VMEM((ROWS, 256), F32),
                pltpu.VMEM((3 * B, 3 * BP), BF16),
                pltpu.VMEM((3 * B, 3 * BP), BF16),
                pltpu.VMEM((NF * FP, 3 * BP), BF16),
                pltpu.VMEM((QP, ROWS), BF16),
                pltpu.VMEM((2 * B, 2 * NF * FP), BF16),
                pltpu.VMEM((3 * BP, Q * E), BF16),
                pltpu.VMEM((3 * B, Q * E), F32),
                pltpu.VMEM((Q, B, E), F32),
                pltpu.VMEM((Q, B, E), F32),
                pltpu.VMEM((ROWS, FACES), F32),
                pltpu.VMEM((ROWS, 2 * FACES), BF16),
                pltpu.VMEM((FACES + slots * cap, FACES), BF16),
                pltpu.VMEM((slots * cap, FACES), BF16),
                pltpu.VMEM((ROWS, FACES), F32),
                pltpu.VMEM((ROWS, FACES), F32),
                pltpu.VMEM((QP, FACES), F32),
                pltpu.VMEM((NF * FP, Q * E), F32),
                pltpu.VMEM((2 * NF * FP, Q * E), BF16),
                pltpu.VMEM((Q, B, E), F32),
                pltpu.VMEM((slots * cap, ROWS), F32),
                pltpu.VMEM((slots * cap, ROWS), F32),
                pltpu.VMEM((slots + 1, 8, E), F32),
                pltpu.VMEM((slots, 8, E), F32),
                pltpu.VMEM((8, E), F32),
                pltpu.VMEM((n_src - 1, 8, E), F32),
                dma,
                dma((slots,)),
                dma((slots,)),
                dma((slots,)),
                dma((slots,)),
                dma((n_src - 1,)),
                dma((n_src - 1,)),
            ],
            compiler_params=pltpu.CompilerParams(
                collective_id=0, has_side_effects=True, vmem_limit_bytes=48 * 1024 * 1024
            ),
        )(
            adj, fwd, star, flux, stiff, restr, rot, lift, kw, nbr, send, orient,
            clus.reshape(1, E), cell.reshape(1, E),
        )

    placed = (
        P("src", None, None, "dom"),
        P("src", None, None, "dom"),
        P(None, None, None, "dom"),
        P(None, None, None, None, "dom"),
        P(),
        P(),
        P(),
        P(),
        P(),
        P(None, "dom"),
        P(None, "dom"),
        P(None, "dom"),
        P("dom"),
        P("dom"),
    )
    return jax.shard_map(
        body,
        mesh=mesh,
        in_specs=placed,
        out_specs=(P("src", None, None, "dom"), P(None, "dom")),
        check_vma=False,
    )
```

profile of v0, /device:TPU:1, one launch (start us, length us, event | category | flops | bytes accessed | tf_op | source)
XLA Modules:
  0.0 37.4 jit_solution(1723745921974797522)
XLA Ops:
  0.6 0.0 copy-start.11
  0.6 0.0 copy-start.9
  0.7 0.0 copy-start.10
  0.7 0.0 copy-start.12
  0.7 0.0 copy-start.13
  0.7 0.6 %copy-done.11 = s32[4,128]{1,0:T(4,128)S(1)} copy-done((s32[4,128]{1,0:T(4,128)S(1)}, s32[4,128]{1,0:T(4,128)}, u32[]{:S(2)}) %copy-start.11) | copy-done | bytes 2072
  1.3 0.0 copy-done.9
  1.3 0.0 copy-done.10
  1.4 0.0 copy-done.12
  1.4 0.0 copy-done.13
  1.4 0.0 copy-start
  1.4 1.0 %copy-done = f32[4,2,9,9,128]{4,1,3,2,0:T(2,128)S(1)} copy-done((f32[4,2,9,9,128]{4,1,3,2,0:T(2,128)S(1)}, f32[4,2,9,9,128]{4,1,3,2,0:T(2,128)}, u32[]{:S(2)}) %copy-start) | copy-done | bytes 331800
  2.3 0.0 copy-start.1
  2.3 0.9 %copy-done.1 = f32[1,9,56,128]{3,2,1,0:T(8,128)S(1)} copy-done((f32[1,9,56,128]{3,2,1,0:T(8,128)S(1)}, f32[1,9,56,128]{3,2,1,0:T(8,128)}, u32[]{:S(2)}) %copy-start.1) | copy-done | bytes 258072
  3.3 0.0 copy-start.2
  3.3 0.9 %copy-done.2 = f32[3,9,9,128]{3,0,2,1:T(4,128)S(1)} copy-done((f32[3,9,9,128]{3,0,2,1:T(4,128)S(1)}, f32[3,9,9,128]{3,0,2,1:T(4,128)}, u32[]{:S(2)}) %copy-start.2) | copy-done | bytes 124440
  4.2 0.0 copy-start.3
  4.2 0.9 %copy-done.3 = bf16[1,9,56,128]{3,2,1,0:T(8,128)(2,1)S(1)} copy-done((bf16[1,9,56,128]{3,2,1,0:T(8,128)(2,1)S(1)}, bf16[1,9,56,128]{3,2,1,0:T(8,128)(2,1)}, u32[]{:S(2)}) %copy-start.3) | copy-done | bytes 129048
  5.1 0.0 copy-start.4
  5.1 0.9 %copy-done.4 = f32[3,56,56]{2,1,0:T(8,128)S(1)} copy-done((f32[3,56,56]{2,1,0:T(8,128)S(1)}, f32[3,56,56]{2,1,0:T(8,128)}, u32[]{:S(2)}) %copy-start.4) | copy-done | bytes 37656
  6.0 0.0 copy-start.5
  6.0 0.8 %copy-done.5 = f32[4,56,21]{1,0,2:T(4,128)S(1)} copy-done((f32[4,56,21]{1,0,2:T(4,128)S(1)}, f32[4,56,21]{1,0,2:T(4,128)}, u32[]{:S(2)}) %copy-start.5) | copy-done | bytes 18840
  6.8 0.0 copy-start.6
  6.8 0.8 %copy-done.6 = f32[4,21,56]{2,0,1:T(4,128)S(1)} copy-done((f32[4,21,56]{2,0,1:T(4,128)S(1)}, f32[4,21,56]{2,0,1:T(4,128)}, u32[]{:S(2)}) %copy-start.6) | copy-done | bytes 18840
  7.6 0.0 copy-start.7
  7.6 0.8 %copy-done.7 = f32[3,21,21]{2,1,0:T(8,128)S(1)} copy-done((f32[3,21,21]{2,1,0:T(8,128)S(1)}, f32[3,21,21]{2,1,0:T(8,128)}, u32[]{:S(2)}) %copy-start.7) | copy-done | bytes 5316
  8.3 0.0 copy-start.8
  8.3 0.7 %copy-done.8 = f32[3,9,9]{2,0,1:T(4,128)S(1)} copy-done((f32[3,9,9]{2,0,1:T(4,128)S(1)}, f32[3,9,9]{2,0,1:T(4,128)}, u32[]{:S(2)}) %copy-start.8) | copy-done | bytes 996
  9.0 27.1 %shard_map.149 = (f32[1,9,56,128]{3,2,1,0:T(8,128)S(1)}, f32[3,128]{1,0:T(4,128)S(1)}) custom-call(f32[1,9,56,128]{3,2,1,0:T(8,128)S(1)} %copy-done.1, bf16[1,9,56,128]{3,2,1,0:T(8,128)(2,1)S(1)} %copy-done.3, f32[9,9,3,128]{3,2,1,0:T(4,128)S(1)} %bitcast.8, f32[4,9,9,2,128]{4,3,2,1,0:T(2,128)S(1)} %bitcast.7, f32[3,56,56]{2,1,0:T(8,128)S(1)} %copy-done.4, ...), custom_call_target="tpu_custom_call" | custom-call | tf_op jit(solution)/shard_map/pallas_call | solution.py:427
  36.2 0.7 %copy.18 = f32[1,9,56,128]{3,2,1,0:T(8,128)} copy(f32[1,9,56,128]{3,2,1,0:T(8,128)S(1)} %get-tuple-element.4) | data formatting | bytes 516096
  36.9 0.6 %copy.19 = f32[3,128]{1,0:T(4,128)} copy(f32[3,128]{1,0:T(4,128)S(1)} %get-tuple-element.5) | data formatting | bytes 3072
Async XLA Ops:
  0.6 0.7 %copy-start.11 = (s32[4,128]{1,0:T(4,128)S(1)}, s32[4,128]{1,0:T(4,128)}, u32[]{:S(2)}) copy-start(s32[4,128]{1,0:T(4,128)} %orient_ref.1) | copy-start | bytes 6148
  0.6 0.7 %copy-start.9 = (s32[6,32]{1,0:T(8,128)S(1)}, s32[6,32]{1,0:T(8,128)}, u32[]{:S(2)}) copy-start(s32[6,32]{1,0:T(8,128)} %send_ref.1) | copy-start | bytes 2308
  0.7 0.7 %copy-start.10 = (s32[4,128]{1,0:T(4,128)S(1)}, s32[4,128]{1,0:T(4,128)}, u32[]{:S(2)}) copy-start(s32[4,128]{1,0:T(4,128)} %nbr_ref.1) | copy-start | bytes 6148
  0.7 0.7 %copy-start.12 = (s32[128]{0:T(128)S(1)}, s32[128]{0:T(128)}, u32[]{:S(2)}) copy-start(s32[128]{0:T(128)} %param.26) | copy-start | bytes 1540
  0.7 0.7 %copy-start.13 = (s32[128]{0:T(128)S(1)}, s32[128]{0:T(128)}, u32[]{:S(2)}) copy-start(s32[128]{0:T(128)} %param.27) | copy-start | bytes 1540
  1.4 1.0 %copy-start = (f32[4,2,9,9,128]{4,1,3,2,0:T(2,128)S(1)}, f32[4,2,9,9,128]{4,1,3,2,0:T(2,128)}, u32[]{:S(2)}) copy-start(f32[4,2,9,9,128]{4,1,3,2,0:T(2,128)} %param.17) | copy-start | bytes 995332
  2.3 0.9 %copy-start.1 = (f32[1,9,56,128]{3,2,1,0:T(8,128)S(1)}, f32[1,9,56,128]{3,2,1,0:T(8,128)}, u32[]{:S(2)}) copy-start(f32[1,9,56,128]{3,2,1,0:T(8,128)} %adj_ref.1) | copy-start | bytes 774148
  3.3 0.9 %copy-start.2 = (f32[3,9,9,128]{3,0,2,1:T(4,128)S(1)}, f32[3,9,9,128]{3,0,2,1:T(4,128)}, u32[]{:S(2)}) copy-start(f32[3,9,9,128]{3,0,2,1:T(4,128)} %param.16) | copy-start | bytes 373252
  4.2 0.9 %copy-start.3 = (bf16[1,9,56,128]{3,2,1,0:T(8,128)(2,1)S(1)}, bf16[1,9,56,128]{3,2,1,0:T(8,128)(2,1)}, u32[]{:S(2)}) copy-start(bf16[1,9,56,128]{3,2,1,0:T(8,128)(2,1)} %fwd_ref.1) | copy-start | bytes 387076
  5.1 0.9 %copy-start.4 = (f32[3,56,56]{2,1,0:T(8,128)S(1)}, f32[3,56,56]{2,1,0:T(8,128)}, u32[]{:S(2)}) copy-start(f32[3,56,56]{2,1,0:T(8,128)} %stiff_ref.1) | copy-start | bytes 112900
  6.0 0.8 %copy-start.5 = (f32[4,56,21]{1,0,2:T(4,128)S(1)}, f32[4,56,21]{1,0,2:T(4,128)}, u32[]{:S(2)}) copy-start(f32[4,56,21]{1,0,2:T(4,128)} %param.19) | copy-start | bytes 56452
  6.8 0.8 %copy-start.6 = (f32[4,21,56]{2,0,1:T(4,128)S(1)}, f32[4,21,56]{2,0,1:T(4,128)}, u32[]{:S(2)}) copy-start(f32[4,21,56]{2,0,1:T(4,128)} %param.21) | copy-start | bytes 56452
  7.6 0.8 %copy-start.7 = (f32[3,21,21]{2,1,0:T(8,128)S(1)}, f32[3,21,21]{2,1,0:T(8,128)}, u32[]{:S(2)}) copy-start(f32[3,21,21]{2,1,0:T(8,128)} %rot_ref.1) | copy-start | bytes 15880
  8.3 0.7 %copy-start.8 = (f32[3,9,9]{2,0,1:T(4,128)S(1)}, f32[3,9,9]{2,0,1:T(4,128)}, u32[]{:S(2)}) copy-start(f32[3,9,9]{2,0,1:T(4,128)} %param.22) | copy-start | bytes 2920
where the time goes:
time: 38 us; the launch traced here: 37.4 us
  Pallas kernels  27.1 us (71%)
  local copies, waits for them, and re-layouts  9.64 us (25%)
  between operations  0.7 us (2%)
    pallas_call x1, Pallas kernels, body(): pl.pallas_call(functools.partial(kernel, n_dom, n_src, reach, cap), out_s...  27.1 us
    unnamed x30, local copies, waits for them, and re-layouts  9.64 us

commit v1 on v0

--- a/solution.py
+++ b/solution.py
@@ -23,6 +23,8 @@
 QP = Q * FP
 PARAMS = 3
 
+ADJ, FWD, STAR, FLUX, STIFF, RESTR, ROT, LIFT, KW, NBR, SEND, ORIENT, CLUS, CELL = range(14)
+
 
 def halves(x):
     high = x.astype(BF16).astype(F32)
@@ -42,23 +44,15 @@
     n_src,
     reach,
     cap,
-    adj_ref,
-    fwd_ref,
-    star_ref,
-    flux_hbm,
-    stiff_ref,
-    restr_ref,
-    rot_ref,
-    lift_ref,
-    kw_ref,
-    nbr_ref,
-    send_ref,
-    orient_ref,
-    clus_ref,
-    cell_ref,
-    out_ref,
-    grad_ref,
-    flux_ref,
+    *refs,
+):
+    inputs, (out_ref, grad_ref), refs = refs[:14], refs[14:16], refs[16:]
+    held, refs = refs[:14], refs[14:]
+    (
+        adj_ref, fwd_ref, star_ref, flux_ref, stiff_ref, restr_ref, rot_ref, lift_ref, kw_ref,
+        nbr_ref, send_ref, orient_ref, clus_ref, cell_ref,
+    ) = held
+    (
     build,
     wk,
     wv,
@@ -85,32 +79,39 @@
     recvwin,
     sendsum,
     recvsum,
-    flux_sem,
+    load_sem,
     send_sem,
     recv_sem,
     wsend_sem,
     wrecv_sem,
     ssend_sem,
     srecv_sem,
-):
+    ) = refs
     dom = lax.axis_index("dom")
     src = lax.axis_index("src")
     slots = 2 * reach
     up = [lax.rem(dom + (k + 1), n_dom) for k in range(reach)]
     down = [lax.rem(dom + (n_dom - k - 1), n_dom) for k in range(reach)]
     partners = up + down
+    present = [dom + (k + 1) < n_dom for k in range(reach)] + [dom >= k + 1 for k in range(reach)]
     others = [lax.rem(src + (s + 1), n_src) for s in range(n_src - 1)]
 
-    flux_copy = pltpu.make_async_copy(flux_hbm, flux_ref, flux_sem)
-    flux_copy.start()
+    loads = [pltpu.make_async_copy(inputs[i], held[i], load_sem.at[i]) for i in range(14)]
+    for i in (STIFF, ADJ, STAR, RESTR, SEND, FWD, KW, CELL, FLUX, NBR, ROT, LIFT, ORIENT, CLUS):
+        loads[i].start()
 
     barrier = pltpu.get_barrier_semaphore()
-    for partner in partners:
-        pl.semaphore_signal(barrier, inc=1, device_id={"dom": partner}, device_id_type=MESH)
+    for k in range(slots):
+
+        @pl.when(present[k])
+        def _():
+            pl.semaphore_signal(barrier, inc=1, device_id={"dom": partners[k]}, device_id_type=MESH)
+
     for other in others:
         pl.semaphore_signal(barrier, inc=1, device_id={"src": other}, device_id_type=MESH)
 
     build[...] = jnp.zeros_like(build)
+    loads[STIFF].wait()
     for d in range(3):
         high, low = halves(stiff_ref[d])
         build[d * B : (d + 1) * B, 0:B] = high
@@ -133,7 +134,9 @@
         put_state(q, value)
         return carry
 
+    loads[ADJ].wait()
     lax.fori_loop(0, Q, start_state, 0)
+    loads[STAR].wait()
 
     def multiply(weights):
         for tile in range(5):
@@ -178,6 +181,7 @@
 
     lax.fori_loop(0, Q, take_integral, 0)
 
+    loads[RESTR].wait()
     build[...] = jnp.zeros_like(build)
     for j in range(NF):
         high, low = halves(restr_ref[:, j, :])
@@ -199,6 +203,7 @@
     pcat[:, 0:FACES] = high.astype(BF16)
     pcat[:, FACES : 2 * FACES] = low.astype(BF16)
 
+    loads[SEND].wait()
     listed = send_ref[...].astype(F32).T
     face_lane = lax.broadcasted_iota(jnp.int32, (cap, FACES), 1).astype(F32)
     for k in range(slots):
@@ -206,7 +211,10 @@
         ohs[k * cap : (k + 1) * cap, :] = jnp.where(hit, 1.0, 0.0).astype(BF16)
     sendbuf[...] = nt_dot(ohs[...], pcat[:, 0:FACES]) + nt_dot(ohs[...], pcat[:, FACES : 2 * FACES])
 
-    pl.semaphore_wait(barrier, 2 * reach + n_src - 1)
+    arrivals = n_src - 1
+    for k in range(slots):
+        arrivals = arrivals + present[k].astype(jnp.int32)
+    pl.semaphore_wait(barrier, arrivals)
 
     def trace_copy(k):
         part = pl.ds(k * cap, cap)
@@ -220,8 +228,14 @@
         )
 
     for k in range(slots):
-        trace_copy(k).start()
-
+
+        @pl.when(present[k])
+        def _():
+            trace_copy(k).start()
+
+
+    for i in (FWD, KW, CELL):
+        loads[i].wait()
     fwd32[...] = fwd_ref[0].astype(F32)
 
     def pair_step(q, carry):
@@ -261,9 +275,14 @@
         )
 
     for k in range(slots):
-        window_copy(k).start()
-
-    flux_copy.wait()
+
+        @pl.when(present[k])
+        def _():
+            window_copy(k).start()
+
+
+    for i in (FLUX, NBR, ROT, LIFT, ORIENT, CLUS):
+        loads[i].wait()
 
     def flux_side(j, side, values, finish):
         lanes = pl.ds(pl.multiple_of(j * E, E), E)
@@ -326,7 +345,15 @@
     lw[...] = build[0 : 2 * B, 0 : 2 * NF * FP].astype(BF16)
 
     for k in range(slots):
-        window_copy(k).wait_recv()
+
+        @pl.when(present[(k + reach) % slots])
+        def _():
+            window_copy(k).wait_recv()
+
+        @pl.when(jnp.logical_not(present[(k + reach) % slots]))
+        def _():
+            recvwin[k] = jnp.zeros((8, E), F32)
+
     total = sendwin[reach]
     for k in range(slots):
         total = total + recvwin[k]
@@ -346,7 +373,15 @@
         sum_copy(s).start()
 
     for k in range(slots):
-        trace_copy(k).wait_recv()
+
+        @pl.when(present[(k + reach) % slots])
+        def _():
+            trace_copy(k).wait_recv()
+
+        @pl.when(jnp.logical_not(present[(k + reach) % slots]))
+        def _():
+            recvbuf[k * cap : (k + 1) * cap] = jnp.zeros((cap, ROWS), F32)
+
     high, low = halves(recvbuf[...].T)
     far = oh[FACES : FACES + slots * cap, :]
     gath[...] = gath[...] + nn_dot(high.astype(BF16), far) + nn_dot(low.astype(BF16), far)
@@ -402,8 +437,12 @@
     grad_ref[...] = total[0:PARAMS]
 
     for k in range(slots):
-        trace_copy(k).wait_send()
-        window_copy(k).wait_send()
+
+        @pl.when(present[k])
+        def _():
+            trace_copy(k).wait_send()
+            window_copy(k).wait_send()
+
     for s in range(n_src - 1):
         sum_copy(s).wait_send()
 
@@ -419,10 +458,11 @@
         lift = lift.transpose(1, 0, 2)
         kw = kw.transpose(1, 0, 2)
         slots = 2 * reach
+        operands = (
+            adj, fwd, star, flux, stiff, restr, rot, lift, kw, nbr, send, orient,
+            clus.reshape(1, E), cell.reshape(1, E),
+        )
         vmem = pl.BlockSpec(memory_space=pltpu.VMEM)
-        specs = [vmem] * 14
-        specs[3] = pl.BlockSpec(memory_space=pl.ANY)
-        specs[8] = pl.BlockSpec(memory_space=pltpu.SMEM)
         dma = pltpu.SemaphoreType.DMA
         return pl.pallas_call(
             functools.partial(kernel, n_dom, n_src, reach, cap),
@@ -430,10 +470,10 @@
                 jax.ShapeDtypeStruct(adj.shape, F32),
                 jax.ShapeDtypeStruct((PARAMS, E), F32),
             ),
-            in_specs=specs,
+            in_specs=[pl.BlockSpec(memory_space=pltpu.HBM)] * 14,
             out_specs=(vmem, vmem),
             scratch_shapes=[
-                pltpu.VMEM(flux.shape, F32),
+                *[(pltpu.SMEM if i == KW else pltpu.VMEM)(x.shape, x.dtype) for i, x in enumerate(operands)],
                 pltpu.VMEM((ROWS, 256), F32),
                 pltpu.VMEM((3 * B, 3 * BP), BF16),
                 pltpu.VMEM((3 * B, 3 * BP), BF16),
@@ -460,7 +500,7 @@
                 pltpu.VMEM((slots, 8, E), F32),
                 pltpu.VMEM((8, E), F32),
                 pltpu.VMEM((n_src - 1, 8, E), F32),
-                dma,
+                dma((14,)),
                 dma((slots,)),
                 dma((slots,)),
                 dma((slots,)),
@@ -469,12 +509,9 @@
                 dma((n_src - 1,)),
             ],
             compiler_params=pltpu.CompilerParams(
-                collective_id=0, has_side_effects=True, vmem_limit_bytes=48 * 1024 * 1024
+                collective_id=0, has_side_effects=True, vmem_limit_bytes=63 * 1024 * 1024
             ),
-        )(
-            adj, fwd, star, flux, stiff, restr, rot, lift, kw, nbr, send, orient,
-            clus.reshape(1, E), cell.reshape(1, E),
-        )
+        )(*operands)
 
     placed = (
         P("src", None, None, "dom"),

time: 38 us -> 28.8 us (0.76)
  the two profiles are of different devices: /device:TPU:1 before, /device:TPU:40 now
where the time goes in v1:
time: 28.8 us; the launch traced here: 28.7 us
  Pallas kernels  25.8 us (90%)
  local copies, waits for them, and re-layouts  2.25 us (8%)
  between operations  0.65 us (2%)
    pallas_call x1, Pallas kernels, body(): pl.pallas_call(functools.partial(kernel, n_dom, n_src, reach, cap), out_s...  25.8 us
    unnamed x4, local copies, waits for them, and re-layouts  2.25 us

profile of v1, /device:TPU:40, one launch (start us, length us, event | category | flops | bytes accessed | tf_op | source)
XLA Modules:
  0.0 28.7 jit_solution(14053087574758997767)
XLA Ops:
  0.6 25.8 %shard_map.149 = (f32[1,9,56,128]{3,2,1,0:T(8,128)}, f32[3,128]{1,0:T(4,128)}) custom-call(f32[1,9,56,128]{3,2,1,0:T(8,128)} %refs_0_.1, bf16[1,9,56,128]{3,2,1,0:T(8,128)(2,1)} %refs_1_.1, f32[9,9,3,128]{3,2,1,0:T(4,128)} %bitcast.8, f32[4,9,9,2,128]{4,3,2,1,0:T(2,128)} %bitcast.7, f32[3,56,56]{2,1,0:T(8,128)} %refs_4_.1, f32[21,4,56]{2,1,0:T(4,128)} %bitcast.9, ...), custom_call_target="tpu_custom_call" | custom-call | tf_op jit(solution)/shard_map/pallas_call | solution.py:467
  26.4 0.0 copy-start
  26.4 1.7 %copy.18 = f32[1,9,56,128]{3,2,1,0:T(8,128)} copy(f32[1,9,56,128]{3,2,1,0:T(8,128)} %get-tuple-element.4) | data formatting | bytes 516096
  28.1 0.0 copy-done
  28.1 0.6 %copy.19 = f32[3,128]{1,0:T(4,128)} copy(f32[3,128]{1,0:T(4,128)S(1)} %copy-done) | data formatting | bytes 3072
Async XLA Ops:
  26.4 1.7 %copy-start = (f32[3,128]{1,0:T(4,128)S(1)}, f32[3,128]{1,0:T(4,128)}, u32[]{:S(2)}) copy-start(f32[3,128]{1,0:T(4,128)} %get-tuple-element.5) | copy-start | bytes 4612

commit v2 on v1

--- a/solution.py
+++ b/solution.py
@@ -77,38 +77,46 @@
     recvbuf,
     sendwin,
     recvwin,
-    sendsum,
-    recvsum,
     load_sem,
     send_sem,
     recv_sem,
     wsend_sem,
     wrecv_sem,
-    ssend_sem,
-    srecv_sem,
     ) = refs
     dom = lax.axis_index("dom")
     src = lax.axis_index("src")
     slots = 2 * reach
-    up = [lax.rem(dom + (k + 1), n_dom) for k in range(reach)]
-    down = [lax.rem(dom + (n_dom - k - 1), n_dom) for k in range(reach)]
-    partners = up + down
-    present = [dom + (k + 1) < n_dom for k in range(reach)] + [dom >= k + 1 for k in range(reach)]
-    others = [lax.rem(src + (s + 1), n_src) for s in range(n_src - 1)]
+    offsets = [o - reach for o in range(2 * reach + 1)]
+    present = [(dom + d >= 0) & (dom + d < n_dom) for d in offsets]
+    sources = [lax.rem(src + s, n_src) for s in range(n_src)]
+    goes = [reach + k + 1 for k in range(reach)] + [reach - k - 1 for k in range(reach)]
+    comes = [2 * reach - o for o in goes]
+    windows = [(o, s) for o in range(2 * reach + 1) for s in range(n_src) if (o, s) != (reach, 0)]
+
+    def for_each(keys, where, action):
+        for o in range(2 * reach + 1):
+            mine = [k for k in keys if where(k) == o]
+            if not mine:
+                continue
+
+            @pl.when(present[o])
+            def _():
+                for k in mine:
+                    action(k)
 
     loads = [pltpu.make_async_copy(inputs[i], held[i], load_sem.at[i]) for i in range(14)]
     for i in (STIFF, ADJ, STAR, RESTR, SEND, FWD, KW, CELL, FLUX, NBR, ROT, LIFT, ORIENT, CLUS):
         loads[i].start()
 
     barrier = pltpu.get_barrier_semaphore()
-    for k in range(slots):
-
-        @pl.when(present[k])
-        def _():
-            pl.semaphore_signal(barrier, inc=1, device_id={"dom": partners[k]}, device_id_type=MESH)
-
-    for other in others:
-        pl.semaphore_signal(barrier, inc=1, device_id={"src": other}, device_id_type=MESH)
+
+    def greet(key):
+        o, s = key
+        pl.semaphore_signal(
+            barrier, inc=1, device_id={"dom": dom + offsets[o], "src": sources[s]}, device_id_type=MESH
+        )
+
+    for_each(windows, lambda key: key[0], greet)
 
     build[...] = jnp.zeros_like(build)
     loads[STIFF].wait()
@@ -174,6 +182,54 @@
         return carry
 
     lax.fori_loop(0, 5, degree_step, 0)
+
+    for i in (FWD, KW, CELL):
+        loads[i].wait()
+    fwd32[...] = fwd_ref[0].astype(F32)
+
+    def pair_step(q, carry):
+        own = integral[q]
+        sums = list(carry)
+        for r in range(Q):
+            product = own * fwd32[r]
+            pair = product[0:8]
+            for c in range(1, 7):
+                pair = pair + product[8 * c : 8 * c + 8]
+            for n in range(PARAMS):
+                sums[n] = sums[n] + kw_ref[q, n, r] * pair
+        return tuple(sums)
+
+    sums = lax.fori_loop(0, Q, pair_step, tuple(jnp.zeros((8, E), F32) for _ in range(PARAMS)))
+    terms = jnp.concatenate(
+        [jnp.sum(s, axis=0, keepdims=True) for s in sums] + [jnp.zeros((8 - PARAMS, E), F32)], axis=0
+    )
+    high, low = halves(terms)
+    both = jnp.concatenate([high, low], axis=0).astype(BF16)
+    place = cell_ref[...] - (dom - reach) * E
+    for o in range(2 * reach + 1):
+        row = lax.broadcasted_iota(jnp.int32, (E, E), 0) + o * E
+        hit = jnp.where(row == place, 1.0, 0.0).astype(BF16)
+        summed = nt_dot(both, hit)
+        sendwin[o] = summed[0:8] + summed[8:16]
+
+    neighbours = -1
+    for here in present:
+        neighbours = neighbours + n_src * here.astype(jnp.int32)
+    pl.semaphore_wait(barrier, neighbours)
+
+    def window_copy(n):
+        o, s = windows[n]
+        return pltpu.make_async_remote_copy(
+            src_ref=sendwin.at[o],
+            dst_ref=recvwin.at[n],
+            send_sem=wsend_sem.at[n],
+            recv_sem=wrecv_sem.at[n],
+            device_id={"dom": dom + offsets[o], "src": sources[s]},
+            device_id_type=MESH,
+        )
+
+    count = range(len(windows))
+    for_each(count, lambda n: windows[n][0], lambda n: window_copy(n).start())
 
     def take_integral(q, carry):
         put_state(q, integral[q])
@@ -211,11 +267,6 @@
         ohs[k * cap : (k + 1) * cap, :] = jnp.where(hit, 1.0, 0.0).astype(BF16)
     sendbuf[...] = nt_dot(ohs[...], pcat[:, 0:FACES]) + nt_dot(ohs[...], pcat[:, FACES : 2 * FACES])
 
-    arrivals = n_src - 1
-    for k in range(slots):
-        arrivals = arrivals + present[k].astype(jnp.int32)
-    pl.semaphore_wait(barrier, arrivals)
-
     def trace_copy(k):
         part = pl.ds(k * cap, cap)
         return pltpu.make_async_remote_copy(
@@ -223,63 +274,11 @@
             dst_ref=recvbuf.at[part],
             send_sem=send_sem.at[k],
             recv_sem=recv_sem.at[k],
-            device_id={"dom": partners[k]},
+            device_id={"dom": dom + offsets[goes[k]]},
             device_id_type=MESH,
         )
 
-    for k in range(slots):
-
-        @pl.when(present[k])
-        def _():
-            trace_copy(k).start()
-
-
-    for i in (FWD, KW, CELL):
-        loads[i].wait()
-    fwd32[...] = fwd_ref[0].astype(F32)
-
-    def pair_step(q, carry):
-        own = integral[q]
-        sums = list(carry)
-        for r in range(Q):
-            product = own * fwd32[r]
-            pair = product[0:8]
-            for c in range(1, 7):
-                pair = pair + product[8 * c : 8 * c + 8]
-            for n in range(PARAMS):
-                sums[n] = sums[n] + kw_ref[q, n, r] * pair
-        return tuple(sums)
-
-    sums = lax.fori_loop(0, Q, pair_step, tuple(jnp.zeros((8, E), F32) for _ in range(PARAMS)))
-    terms = jnp.concatenate(
-        [jnp.sum(s, axis=0, keepdims=True) for s in sums] + [jnp.zeros((8 - PARAMS, E), F32)], axis=0
-    )
-    high, low = halves(terms)
-    both = jnp.concatenate([high, low], axis=0).astype(BF16)
-    place = cell_ref[...] - (dom - reach) * E
-    for o in range(2 * reach + 1):
-        row = lax.broadcasted_iota(jnp.int32, (E, E), 0) + o * E
-        hit = jnp.where(row == place, 1.0, 0.0).astype(BF16)
-        summed = nt_dot(both, hit)
-        sendwin[o] = summed[0:8] + summed[8:16]
-
-    def window_copy(k):
-        o = reach + k + 1 if k < reach else 2 * reach - 1 - k
-        return pltpu.make_async_remote_copy(
-            src_ref=sendwin.at[o],
-            dst_ref=recvwin.at[k],
-            send_sem=wsend_sem.at[k],
-            recv_sem=wrecv_sem.at[k],
-            device_id={"dom": partners[k]},
-            device_id_type=MESH,
-        )
-
-    for k in range(slots):
-
-        @pl.when(present[k])
-        def _():
-            window_copy(k).start()
-
+    for_each(range(slots), lambda k: goes[k], lambda k: trace_copy(k).start())
 
     for i in (FLUX, NBR, ROT, LIFT, ORIENT, CLUS):
         loads[i].wait()
@@ -344,43 +343,15 @@
         build[B : 2 * B, j * FP : j * FP + F] = low
     lw[...] = build[0 : 2 * B, 0 : 2 * NF * FP].astype(BF16)
 
+    def no_faces(k):
+        recvbuf[k * cap : (k + 1) * cap] = jnp.zeros((cap, ROWS), F32)
+
+    for_each(range(slots), lambda k: comes[k], lambda k: trace_copy(k).wait_recv())
     for k in range(slots):
 
-        @pl.when(present[(k + reach) % slots])
+        @pl.when(jnp.logical_not(present[comes[k]]))
         def _():
-            window_copy(k).wait_recv()
-
-        @pl.when(jnp.logical_not(present[(k + reach) % slots]))
-        def _():
-            recvwin[k] = jnp.zeros((8, E), F32)
-
-    total = sendwin[reach]
-    for k in range(slots):
-        total = total + recvwin[k]
-    sendsum[...] = total
-
-    def sum_copy(s):
-        return pltpu.make_async_remote_copy(
-            src_ref=sendsum,
-            dst_ref=recvsum.at[s],
-            send_sem=ssend_sem.at[s],
-            recv_sem=srecv_sem.at[s],
-            device_id={"src": others[s]},
-            device_id_type=MESH,
-        )
-
-    for s in range(n_src - 1):
-        sum_copy(s).start()
-
-    for k in range(slots):
-
-        @pl.when(present[(k + reach) % slots])
-        def _():
-            trace_copy(k).wait_recv()
-
-        @pl.when(jnp.logical_not(present[(k + reach) % slots]))
-        def _():
-            recvbuf[k * cap : (k + 1) * cap] = jnp.zeros((cap, ROWS), F32)
+            no_faces(k)
 
     high, low = halves(recvbuf[...].T)
     far = oh[FACES : FACES + slots * cap, :]
@@ -429,22 +400,36 @@
             p = 2 * tile + i
             out_ref[0, p] = jnp.where(moves, base[p] - surface[:, i * E : (i + 1) * E], adj_ref[0, p])
 
-    for s in range(n_src - 1):
-        sum_copy(s).wait_recv()
-    total = sendsum[...]
-    for s in range(n_src - 1):
-        total = total + recvsum[s]
+    def no_window(n):
+        recvwin[n] = jnp.zeros((8, E), F32)
+
+    for_each(count, lambda n: 2 * reach - windows[n][0], lambda n: window_copy(n).wait_recv())
+    for o in range(2 * reach + 1):
+
+        @pl.when(jnp.logical_not(present[2 * reach - o]))
+        def _():
+            for n in count:
+                if windows[n][0] == o:
+                    no_window(n)
+
+    total = sendwin[reach]
+    for n in count:
+        total = total + recvwin[n]
     grad_ref[...] = total[0:PARAMS]
 
-    for k in range(slots):
-
-        @pl.when(present[k])
-        def _():
-            trace_copy(k).wait_send()
-            window_copy(k).wait_send()
-
-    for s in range(n_src - 1):
-        sum_copy(s).wait_send()
+    for_each(range(slots), lambda k: goes[k], lambda k: trace_copy(k).wait_send())
+    for_each(count, lambda n: windows[n][0], lambda n: window_copy(n).wait_send())
+
+
+def store(next_ref, sums_ref, out_ref, grad_ref, sem):
+    copies = [
+        pltpu.make_async_copy(next_ref, out_ref, sem.at[0]),
+        pltpu.make_async_copy(sums_ref, grad_ref, sem.at[1]),
+    ]
+    for copy in copies:
+        copy.start()
+    for copy in copies:
+        copy.wait()
 
 
 def solution(mesh):
@@ -458,17 +443,19 @@
         lift = lift.transpose(1, 0, 2)
         kw = kw.transpose(1, 0, 2)
         slots = 2 * reach
+        others = (slots + 1) * n_src - 1
         operands = (
             adj, fwd, star, flux, stiff, restr, rot, lift, kw, nbr, send, orient,
             clus.reshape(1, E), cell.reshape(1, E),
         )
         vmem = pl.BlockSpec(memory_space=pltpu.VMEM)
         dma = pltpu.SemaphoreType.DMA
-        return pl.pallas_call(
+        operands = tuple(pltpu.with_memory_space_constraint(x, pltpu.HBM) for x in operands)
+        results = pl.pallas_call(
             functools.partial(kernel, n_dom, n_src, reach, cap),
             out_shape=(
-                jax.ShapeDtypeStruct(adj.shape, F32),
-                jax.ShapeDtypeStruct((PARAMS, E), F32),
+                pltpu.VMEM(adj.shape, F32),
+                pltpu.VMEM((PARAMS, E), F32),
             ),
             in_specs=[pl.BlockSpec(memory_space=pltpu.HBM)] * 14,
             out_specs=(vmem, vmem),
@@ -497,21 +484,28 @@
                 pltpu.VMEM((slots * cap, ROWS), F32),
                 pltpu.VMEM((slots * cap, ROWS), F32),
                 pltpu.VMEM((slots + 1, 8, E), F32),
-                pltpu.VMEM((slots, 8, E), F32),
-                pltpu.VMEM((8, E), F32),
-                pltpu.VMEM((n_src - 1, 8, E), F32),
+                pltpu.VMEM((others, 8, E), F32),
                 dma((14,)),
                 dma((slots,)),
                 dma((slots,)),
-                dma((slots,)),
-                dma((slots,)),
-                dma((n_src - 1,)),
-                dma((n_src - 1,)),
+                dma((others,)),
+                dma((others,)),
             ],
             compiler_params=pltpu.CompilerParams(
-                collective_id=0, has_side_effects=True, vmem_limit_bytes=63 * 1024 * 1024
+                collective_id=0, has_side_effects=True, vmem_limit_bytes=32 * 1024 * 1024
             ),
         )(*operands)
+        return pl.pallas_call(
+            store,
+            out_shape=(
+                jax.ShapeDtypeStruct(adj.shape, F32),
+                jax.ShapeDtypeStruct((PARAMS, E), F32),
+            ),
+            in_specs=[vmem, vmem],
+            out_specs=[pl.BlockSpec(memory_space=pltpu.HBM)] * 2,
+            scratch_shapes=[dma((2,))],
+            compiler_params=pltpu.CompilerParams(vmem_limit_bytes=1024 * 1024),
+        )(*(pltpu.with_memory_space_constraint(x, pltpu.VMEM) for x in results))
 
     placed = (
         P("src", None, None, "dom"),

time: 28.8 us -> 24.6 us (0.85)
  the two profiles are of different devices: /device:TPU:40 before, /device:TPU:57 now
where the time goes in v2:
time: 24.6 us; the launch traced here: 24.4 us
  Pallas kernels  23.8 us (97%)
  between operations  0.64 us (3%)
    pallas_call x1, Pallas kernels, body(): pl.pallas_call(functools.partial(kernel, n_dom, n_src, reach, cap), out_s...  23 us
    pallas_call x1, Pallas kernels, body(): pl.pallas_call(store, out_shape=(jax.ShapeDtypeStruct(adj.shape, F32), ja...  0.72 us

profile of v2, /device:TPU:57, one launch (start us, length us, event | category | flops | bytes accessed | tf_op | source)
XLA Modules:
  0.0 24.4 jit_solution(13146229296549942947)
XLA Ops:
  0.6 23.0 %shard_map.149 = (f32[1,9,56,128]{3,2,1,0:T(8,128)S(1)}, f32[3,128]{1,0:T(4,128)S(1)}) custom-call(f32[1,9,56,128]{3,2,1,0:T(8,128)} %refs_0_.1, bf16[1,9,56,128]{3,2,1,0:T(8,128)(2,1)} %refs_1_.1, f32[9,9,3,128]{3,2,1,0:T(4,128)} %bitcast.8, f32[4,9,9,2,128]{4,3,2,1,0:T(2,128)} %bitcast.7, f32[3,56,56]{2,1,0:T(8,128)} %refs_4_.1, f32[21,4,56]{2,1,0:T(4,128)} %bitcast.9, ...), custom_call_target="tpu_custom_call" | custom-call | tf_op jit(solution)/shard_map/pallas_call | solution.py:454
  23.7 0.7 %shard_map.150 = (f32[1,9,56,128]{3,2,1,0:T(8,128)}, f32[3,128]{1,0:T(4,128)}) custom-call(f32[1,9,56,128]{3,2,1,0:T(8,128)S(1)} %get-tuple-element.4.next_ref, f32[3,128]{1,0:T(4,128)S(1)} %get-tuple-element.5.sums_ref), custom_call_target="tpu_custom_call" | custom-call | tf_op jit(solution)/shard_map/pallas_call | solution.py:498

commit v3 on v2

--- a/solution.py
+++ b/solution.py
@@ -60,7 +60,8 @@
     rb,
     lw,
     v3,
-    applied,
+    even,
+    odd,
     integral,
     fwd32,
     pool,
@@ -105,7 +106,7 @@
                     action(k)
 
     loads = [pltpu.make_async_copy(inputs[i], held[i], load_sem.at[i]) for i in range(14)]
-    for i in (STIFF, ADJ, STAR, RESTR, SEND, FWD, KW, CELL, FLUX, NBR, ROT, LIFT, ORIENT, CLUS):
+    for i in (STIFF, RESTR, SEND, ADJ, STAR, FWD, KW, CELL, FLUX, NBR, ROT, LIFT, ORIENT, CLUS):
         loads[i].start()
 
     barrier = pltpu.get_barrier_semaphore()
@@ -127,6 +128,21 @@
         build[d * B : (d + 1) * B, 2 * BP : 2 * BP + B] = low
     wk[...] = build[0 : 3 * B, 0 : 3 * BP].astype(BF16)
 
+    loads[RESTR].wait()
+    build[...] = jnp.zeros_like(build)
+    for j in range(NF):
+        high, low = halves(restr_ref[:, j, :])
+        build[j * FP : j * FP + F, 0:B] = high
+        build[j * FP : j * FP + F, BP : BP + B] = high
+        build[j * FP : j * FP + F, 2 * BP : 2 * BP + B] = low
+    wt[...] = build[0 : NF * FP, 0 : 3 * BP].astype(BF16)
+    loads[SEND].wait()
+    listed = send_ref[...].astype(F32).T
+    face_lane = lax.broadcasted_iota(jnp.int32, (cap, FACES), 1).astype(F32)
+    for k in range(slots):
+        hit = listed[:, k : k + 1] == face_lane
+        ohs[k * cap : (k + 1) * cap, :] = jnp.where(hit, 1.0, 0.0).astype(BF16)
+
     zeros8 = jnp.zeros((BP - B, E), F32)
 
     def put_state(q, value):
@@ -146,42 +162,48 @@
     lax.fori_loop(0, Q, start_state, 0)
     loads[STAR].wait()
 
-    def multiply(weights):
-        for tile in range(5):
-            lanes = slice(tile * 256, min(tile * 256 + 256, Q * E))
-            applied[:, lanes] = nn_dot(weights[...], v3[:, lanes])
-
-    def contract(block, finish):
-        p0 = block * 3
+    def multiply(weights, group, target):
+        lanes = pl.ds(pl.multiple_of(group * 3 * E, E), 3 * E)
+        target[group] = nn_dot(weights[...], v3[:, lanes])
+
+    def contract(block, source, finish):
         totals = [None] * 3
         for q in range(Q):
             for d in range(3):
-                a = applied[d * B : (d + 1) * B, q * E : (q + 1) * E]
+                a = source[q // 3, d * B : (d + 1) * B, (q % 3) * E : (q % 3 + 1) * E]
                 for i in range(3):
-                    term = star_ref[p0 + i, q, d : d + 1, :] * a
+                    term = star_ref[3 * block + i, q, d : d + 1, :] * a
                     totals[i] = term if totals[i] is None else totals[i] + term
         for i in range(3):
-            finish(p0 + i, totals[i])
-
-    def degree_step(k, carry):
-        multiply(wk)
-        scale = jnp.float32(-1.0 / 6.0)
-        for n in range(4):
-            scale = jnp.where(k == n, jnp.float32(-1.0 / (n + 2)), scale)
-
+            finish(3 * block + i, totals[i])
+
+    def degree_step(scale, now, later):
         def finish(p, total):
             value = total * scale
             integral[p] = integral[p] + value
-            put_state(p, value)
+            put_state(p, integral[p] if later is None else value)
+
+        multiply(wk, 2, now)
+        contract(0, now, finish)
 
         def block_step(block, c):
-            contract(block, finish)
+            if later is not None:
+                multiply(wk, block - 1, later)
+            contract(block, now, finish)
             return c
 
-        lax.fori_loop(0, 3, block_step, 0)
+        lax.fori_loop(1, 3, block_step, 0)
+
+    multiply(wk, 0, even)
+    multiply(wk, 1, even)
+
+    def two_degrees(k, carry):
+        degree_step(jnp.where(k == 0, jnp.float32(-1 / 2), jnp.float32(-1 / 4)), even, odd)
+        degree_step(jnp.where(k == 0, jnp.float32(-1 / 3), jnp.float32(-1 / 5)), odd, even)
         return carry
 
-    lax.fori_loop(0, 5, degree_step, 0)
+    lax.fori_loop(0, 2, two_degrees, 0)
+    degree_step(jnp.float32(-1 / 6), even, None)
 
     for i in (FWD, KW, CELL):
         loads[i].wait()
@@ -210,7 +232,7 @@
         row = lax.broadcasted_iota(jnp.int32, (E, E), 0) + o * E
         hit = jnp.where(row == place, 1.0, 0.0).astype(BF16)
         summed = nt_dot(both, hit)
-        sendwin[o] = summed[0:8] + summed[8:16]
+        sendwin[o] = (summed[0:8] + summed[8:16])[0:PARAMS]
 
     neighbours = -1
     for here in present:
@@ -231,20 +253,6 @@
     count = range(len(windows))
     for_each(count, lambda n: windows[n][0], lambda n: window_copy(n).start())
 
-    def take_integral(q, carry):
-        put_state(q, integral[q])
-        return carry
-
-    lax.fori_loop(0, Q, take_integral, 0)
-
-    loads[RESTR].wait()
-    build[...] = jnp.zeros_like(build)
-    for j in range(NF):
-        high, low = halves(restr_ref[:, j, :])
-        build[j * FP : j * FP + F, 0:B] = high
-        build[j * FP : j * FP + F, BP : BP + B] = high
-        build[j * FP : j * FP + F, 2 * BP : 2 * BP + B] = low
-    wt[...] = build[0 : NF * FP, 0 : 3 * BP].astype(BF16)
     pool[QP:ROWS, :] = jnp.zeros((ROWS - QP, FACES), F32)
     for tile in range(5):
         wide = min(2, Q - 2 * tile)
@@ -259,12 +267,6 @@
     pcat[:, 0:FACES] = high.astype(BF16)
     pcat[:, FACES : 2 * FACES] = low.astype(BF16)
 
-    loads[SEND].wait()
-    listed = send_ref[...].astype(F32).T
-    face_lane = lax.broadcasted_iota(jnp.int32, (cap, FACES), 1).astype(F32)
-    for k in range(slots):
-        hit = listed[:, k : k + 1] == face_lane
-        ohs[k * cap : (k + 1) * cap, :] = jnp.where(hit, 1.0, 0.0).astype(BF16)
     sendbuf[...] = nt_dot(ohs[...], pcat[:, 0:FACES]) + nt_dot(ohs[...], pcat[:, FACES : 2 * FACES])
 
     def trace_copy(k):
@@ -309,13 +311,14 @@
         build[d * B : (d + 1) * B, BP : BP + B] = high
         build[d * B : (d + 1) * B, 2 * BP : 2 * BP + B] = low
     wv[...] = build[0 : 3 * B, 0 : 3 * BP].astype(BF16)
-    multiply(wv)
+    for group in range(3):
+        multiply(wv, group, odd)
 
     def volume_step(block, carry):
         def finish(p, total):
             base[p] = adj_ref[0, p] + total
 
-        contract(block, finish)
+        contract(block, odd, finish)
         return carry
 
     lax.fori_loop(0, 3, volume_step, 0)
@@ -401,7 +404,7 @@
             out_ref[0, p] = jnp.where(moves, base[p] - surface[:, i * E : (i + 1) * E], adj_ref[0, p])
 
     def no_window(n):
-        recvwin[n] = jnp.zeros((8, E), F32)
+        recvwin[n] = jnp.zeros((PARAMS, E), F32)
 
     for_each(count, lambda n: 2 * reach - windows[n][0], lambda n: window_copy(n).wait_recv())
     for o in range(2 * reach + 1):
@@ -415,7 +418,7 @@
     total = sendwin[reach]
     for n in count:
         total = total + recvwin[n]
-    grad_ref[...] = total[0:PARAMS]
+    grad_ref[...] = total
 
     for_each(range(slots), lambda k: goes[k], lambda k: trace_copy(k).wait_send())
     for_each(count, lambda n: windows[n][0], lambda n: window_copy(n).wait_send())
@@ -468,7 +471,8 @@
                 pltpu.VMEM((QP, ROWS), BF16),
                 pltpu.VMEM((2 * B, 2 * NF * FP), BF16),
                 pltpu.VMEM((3 * BP, Q * E), BF16),
-                pltpu.VMEM((3 * B, Q * E), F32),
+                pltpu.VMEM((3, 3 * B, 3 * E), F32),
+                pltpu.VMEM((3, 3 * B, 3 * E), F32),
                 pltpu.VMEM((Q, B, E), F32),
                 pltpu.VMEM((Q, B, E), F32),
                 pltpu.VMEM((ROWS, FACES), F32),
@@ -483,8 +487,8 @@
                 pltpu.VMEM((Q, B, E), F32),
                 pltpu.VMEM((slots * cap, ROWS), F32),
                 pltpu.VMEM((slots * cap, ROWS), F32),
-                pltpu.VMEM((slots + 1, 8, E), F32),
-                pltpu.VMEM((others, 8, E), F32),
+                pltpu.VMEM((slots + 1, PARAMS, E), F32),
+                pltpu.VMEM((others, PARAMS, E), F32),
                 dma((14,)),
                 dma((slots,)),
                 dma((slots,)),

time: 24.6 us -> 24.2 us (0.984)
  Pallas kernels: 23.8 us -> 23.4 us
    pallas_call x1, Pallas kernels: 23 us -> 22.7 us  [body(): pl.pallas_call(functools.partial(kernel, n_dom, n_src, reach, cap), out_s...]
where the time goes in v3:
time: 24.2 us; the launch traced here: 24 us
  Pallas kernels  23.4 us (97%)
  between operations  0.64 us (3%)
    pallas_call x1, Pallas kernels, body(): pl.pallas_call(functools.partial(kernel, n_dom, n_src, reach, cap), out_s...  22.7 us
    pallas_call x1, Pallas kernels, body(): pl.pallas_call(store, out_shape=(jax.ShapeDtypeStruct(adj.shape, F32), ja...  0.72 us

profile of v3, /device:TPU:57, one launch (start us, length us, event | category | flops | bytes accessed | tf_op | source)
XLA Modules:
  0.0 24.0 jit_solution(14543424870716914580)
XLA Ops:
  0.6 22.7 %shard_map.149 = (f32[1,9,56,128]{3,2,1,0:T(8,128)S(1)}, f32[3,128]{1,0:T(4,128)S(1)}) custom-call(f32[1,9,56,128]{3,2,1,0:T(8,128)} %refs_0_.1, bf16[1,9,56,128]{3,2,1,0:T(8,128)(2,1)} %refs_1_.1, f32[9,9,3,128]{3,2,1,0:T(4,128)} %bitcast.8, f32[4,9,9,2,128]{4,3,2,1,0:T(2,128)} %bitcast.7, f32[3,56,56]{2,1,0:T(8,128)} %refs_4_.1, f32[21,4,56]{2,1,0:T(4,128)} %bitcast.9, ...), custom_call_target="tpu_custom_call" | custom-call | tf_op jit(solution)/shard_map/pallas_call | solution.py:457
  23.3 0.7 %shard_map.150 = (f32[1,9,56,128]{3,2,1,0:T(8,128)}, f32[3,128]{1,0:T(4,128)}) custom-call(f32[1,9,56,128]{3,2,1,0:T(8,128)S(1)} %get-tuple-element.4.next_ref, f32[3,128]{1,0:T(4,128)S(1)} %get-tuple-element.5.sums_ref), custom_call_target="tpu_custom_call" | custom-call | tf_op jit(solution)/shard_map/pallas_call | solution.py:502

commit v4 on v3

--- a/solution.py
+++ b/solution.py
@@ -68,6 +68,7 @@
     pcat,
     oh,
     ohs,
+    ohc,
     gath,
     xg,
     turned,
@@ -95,7 +96,7 @@
     windows = [(o, s) for o in range(2 * reach + 1) for s in range(n_src) if (o, s) != (reach, 0)]
 
     def for_each(keys, where, action):
-        for o in range(2 * reach + 1):
+        for o in reversed(range(2 * reach + 1)):
             mine = [k for k in keys if where(k) == o]
             if not mine:
                 continue
@@ -106,7 +107,7 @@
                     action(k)
 
     loads = [pltpu.make_async_copy(inputs[i], held[i], load_sem.at[i]) for i in range(14)]
-    for i in (STIFF, RESTR, SEND, ADJ, STAR, FWD, KW, CELL, FLUX, NBR, ROT, LIFT, ORIENT, CLUS):
+    for i in (STIFF, ADJ, STAR, RESTR, SEND, CELL):
         loads[i].start()
 
     barrier = pltpu.get_barrier_semaphore()
@@ -142,6 +143,10 @@
     for k in range(slots):
         hit = listed[:, k : k + 1] == face_lane
         ohs[k * cap : (k + 1) * cap, :] = jnp.where(hit, 1.0, 0.0).astype(BF16)
+    loads[CELL].wait()
+    place = cell_ref[...] - (dom - reach) * E
+    row = lax.broadcasted_iota(jnp.int32, ((2 * reach + 1) * E, E), 0)
+    ohc[...] = jnp.where(row == place, 1.0, 0.0).astype(BF16)
 
     zeros8 = jnp.zeros((BP - B, E), F32)
 
@@ -161,6 +166,8 @@
     loads[ADJ].wait()
     lax.fori_loop(0, Q, start_state, 0)
     loads[STAR].wait()
+    for i in (FWD, KW, FLUX, NBR, ROT, LIFT, ORIENT, CLUS):
+        loads[i].start()
 
     def multiply(weights, group, target):
         lanes = pl.ds(pl.multiple_of(group * 3 * E, E), 3 * E)
@@ -205,7 +212,7 @@
     lax.fori_loop(0, 2, two_degrees, 0)
     degree_step(jnp.float32(-1 / 6), even, None)
 
-    for i in (FWD, KW, CELL):
+    for i in (FWD, KW):
         loads[i].wait()
     fwd32[...] = fwd_ref[0].astype(F32)
 
@@ -227,13 +234,10 @@
     )
     high, low = halves(terms)
     both = jnp.concatenate([high, low], axis=0).astype(BF16)
-    place = cell_ref[...] - (dom - reach) * E
+    summed = nt_dot(both, ohc[...])
+    summed = (summed[0:8] + summed[8:16])[0:PARAMS]
     for o in range(2 * reach + 1):
-        row = lax.broadcasted_iota(jnp.int32, (E, E), 0) + o * E
-        hit = jnp.where(row == place, 1.0, 0.0).astype(BF16)
-        summed = nt_dot(both, hit)
-        sendwin[o] = (summed[0:8] + summed[8:16])[0:PARAMS]
-
+        sendwin[o] = summed[:, o * E : (o + 1) * E]
     neighbours = -1
     for here in present:
         neighbours = neighbours + n_src * here.astype(jnp.int32)
@@ -251,7 +255,9 @@
         )
 
     count = range(len(windows))
-    for_each(count, lambda n: windows[n][0], lambda n: window_copy(n).start())
+    rising = [n for n in count if windows[n][0] >= reach]
+    falling = [n for n in count if windows[n][0] < reach]
+    for_each(rising, lambda n: windows[n][0], lambda n: window_copy(n).start())
 
     pool[QP:ROWS, :] = jnp.zeros((ROWS - QP, FACES), F32)
     for tile in range(5):
@@ -281,6 +287,7 @@
         )
 
     for_each(range(slots), lambda k: goes[k], lambda k: trace_copy(k).start())
+    for_each(falling, lambda n: windows[n][0], lambda n: window_copy(n).start())
 
     for i in (FLUX, NBR, ROT, LIFT, ORIENT, CLUS):
         loads[i].wait()
@@ -479,6 +486,7 @@
                 pltpu.VMEM((ROWS, 2 * FACES), BF16),
                 pltpu.VMEM((FACES + slots * cap, FACES), BF16),
                 pltpu.VMEM((slots * cap, FACES), BF16),
+                pltpu.VMEM(((slots + 1) * E, E), BF16),
                 pltpu.VMEM((ROWS, FACES), F32),
                 pltpu.VMEM((ROWS, FACES), F32),
                 pltpu.VMEM((QP, FACES), F32),

time: 24.2 us -> 23.9 us (0.988)
  Pallas kernels: 23.4 us -> 23 us
    pallas_call x1, Pallas kernels: 22.7 us -> 22.2 us  [body(): pl.pallas_call(functools.partial(kernel, n_dom, n_src, reach, cap), out_s...]
where the time goes in v4:
time: 23.9 us; the launch traced here: 23.6 us
  Pallas kernels  23 us (96%)
  between operations  0.64 us (3%)
    pallas_call x1, Pallas kernels, body(): pl.pallas_call(functools.partial(kernel, n_dom, n_src, reach, cap), out_s...  22.2 us
    pallas_call x1, Pallas kernels, body(): pl.pallas_call(store, out_shape=(jax.ShapeDtypeStruct(adj.shape, F32), ja...  0.72 us

profile of v4, /device:TPU:57, one launch (start us, length us, event | category | flops | bytes accessed | tf_op | source)
XLA Modules:
  0.0 23.6 jit_solution(2317942736637419425)
XLA Ops:
  0.6 22.2 %shard_map.149 = (f32[1,9,56,128]{3,2,1,0:T(8,128)S(1)}, f32[3,128]{1,0:T(4,128)S(1)}) custom-call(f32[1,9,56,128]{3,2,1,0:T(8,128)} %refs_0_.1, bf16[1,9,56,128]{3,2,1,0:T(8,128)(2,1)} %refs_1_.1, f32[9,9,3,128]{3,2,1,0:T(4,128)} %bitcast.8, f32[4,9,9,2,128]{4,3,2,1,0:T(2,128)} %bitcast.7, f32[3,56,56]{2,1,0:T(8,128)} %refs_4_.1, f32[21,4,56]{2,1,0:T(4,128)} %bitcast.9, ...), custom_call_target="tpu_custom_call" | custom-call | tf_op jit(solution)/shard_map/pallas_call | solution.py:464
  22.9 0.7 %shard_map.150 = (f32[1,9,56,128]{3,2,1,0:T(8,128)}, f32[3,128]{1,0:T(4,128)}) custom-call(f32[1,9,56,128]{3,2,1,0:T(8,128)S(1)} %get-tuple-element.4.next_ref, f32[3,128]{1,0:T(4,128)S(1)} %get-tuple-element.5.sums_ref), custom_call_target="tpu_custom_call" | custom-call | tf_op jit(solution)/shard_map/pallas_call | solution.py:510

commit v5 on v4

--- a/solution.py
+++ b/solution.py
@@ -142,7 +142,9 @@
     face_lane = lax.broadcasted_iota(jnp.int32, (cap, FACES), 1).astype(F32)
     for k in range(slots):
         hit = listed[:, k : k + 1] == face_lane
-        ohs[k * cap : (k + 1) * cap, :] = jnp.where(hit, 1.0, 0.0).astype(BF16)
+        hit = jnp.where(hit, 1.0, 0.0).astype(BF16)
+        ohs[k * cap : (k + 1) * cap, 0:FACES] = hit
+        ohs[k * cap : (k + 1) * cap, FACES : 2 * FACES] = hit
     loads[CELL].wait()
     place = cell_ref[...] - (dom - reach) * E
     row = lax.broadcasted_iota(jnp.int32, ((2 * reach + 1) * E, E), 0)
@@ -255,8 +257,8 @@
         )
 
     count = range(len(windows))
-    rising = [n for n in count if windows[n][0] >= reach]
-    falling = [n for n in count if windows[n][0] < reach]
+    rising = [n for n in count if windows[n][0] > reach]
+    falling = [n for n in count if windows[n][0] <= reach]
     for_each(rising, lambda n: windows[n][0], lambda n: window_copy(n).start())
 
     pool[QP:ROWS, :] = jnp.zeros((ROWS - QP, FACES), F32)
@@ -273,7 +275,7 @@
     pcat[:, 0:FACES] = high.astype(BF16)
     pcat[:, FACES : 2 * FACES] = low.astype(BF16)
 
-    sendbuf[...] = nt_dot(ohs[...], pcat[:, 0:FACES]) + nt_dot(ohs[...], pcat[:, FACES : 2 * FACES])
+    sendbuf[...] = nt_dot(ohs[...], pcat[...])
 
     def trace_copy(k):
         part = pl.ds(k * cap, cap)
@@ -485,7 +487,7 @@
                 pltpu.VMEM((ROWS, FACES), F32),
                 pltpu.VMEM((ROWS, 2 * FACES), BF16),
                 pltpu.VMEM((FACES + slots * cap, FACES), BF16),
-                pltpu.VMEM((slots * cap, FACES), BF16),
+                pltpu.VMEM((slots * cap, 2 * FACES), BF16),
                 pltpu.VMEM(((slots + 1) * E, E), BF16),
                 pltpu.VMEM((ROWS, FACES), F32),
                 pltpu.VMEM((ROWS, FACES), F32),

time: 23.9 us -> 23.8 us (level)
  no operation moved by 1% of the time
where the time goes in v5:
time: 23.8 us; the launch traced here: 23.6 us
  Pallas kernels  22.9 us (96%)
  between operations  0.64 us (3%)
    pallas_call x1, Pallas kernels, body(): pl.pallas_call(functools.partial(kernel, n_dom, n_src, reach, cap), out_s...  22.2 us
    pallas_call x1, Pallas kernels, body(): pl.pallas_call(store, out_shape=(jax.ShapeDtypeStruct(adj.shape, F32), ja...  0.72 us

profile of v5, /device:TPU:57, one launch (start us, length us, event | category | flops | bytes accessed | tf_op | source)
XLA Modules:
  0.0 23.6 jit_solution(17160524017265162728)
XLA Ops:
  0.6 22.2 %shard_map.149 = (f32[1,9,56,128]{3,2,1,0:T(8,128)S(1)}, f32[3,128]{1,0:T(4,128)S(1)}) custom-call(f32[1,9,56,128]{3,2,1,0:T(8,128)} %refs_0_.1, bf16[1,9,56,128]{3,2,1,0:T(8,128)(2,1)} %refs_1_.1, f32[9,9,3,128]{3,2,1,0:T(4,128)} %bitcast.8, f32[4,9,9,2,128]{4,3,2,1,0:T(2,128)} %bitcast.7, f32[3,56,56]{2,1,0:T(8,128)} %refs_4_.1, f32[21,4,56]{2,1,0:T(4,128)} %bitcast.9, ...), custom_call_target="tpu_custom_call" | custom-call | tf_op jit(solution)/shard_map/pallas_call | solution.py:466
  22.9 0.7 %shard_map.150 = (f32[1,9,56,128]{3,2,1,0:T(8,128)}, f32[3,128]{1,0:T(4,128)}) custom-call(f32[1,9,56,128]{3,2,1,0:T(8,128)S(1)} %get-tuple-element.4.next_ref, f32[3,128]{1,0:T(4,128)S(1)} %get-tuple-element.5.sums_ref), custom_call_target="tpu_custom_call" | custom-call | tf_op jit(solution)/shard_map/pallas_call | solution.py:512
